TPU v7x, 32 devices: a whole 2x2x4 slice. The times are simulated.
32 devices in a mesh: seq: 8 (over z, y), tp: 4 (over x, core).
Axes of the slice: x: 2, y: 2, z: 4, core: 2. Of those that a mesh axis runs over, the one named last changes fastest.
Arguments:
- tokens: bfloat16 [64, 1152], P('seq'), may hold values from -6 to 6
- attn_gain: float32 [1152], replicated, may hold values from 0.1 to 1.9
- w_query: bfloat16 [1152, 1280], P(None, 'tp'), may hold values from -0.1875 to 0.1875
- w_key: bfloat16 [1152, 384], replicated, may hold values from -0.1875 to 0.1875
- w_value: bfloat16 [1152, 384], replicated, may hold values from -0.1875 to 0.1875
- w_out: bfloat16 [1280, 1152], P('tp'), may hold values from -0.1875 to 0.1875
- prefix_keys: bfloat16 [8, 4096, 384], P(None, 'seq'), may hold values from -92 to 92
- prefix_values: bfloat16 [8, 4096, 384], P(None, 'seq'), may hold values from -6 to 6
- suffix_keys: bfloat16 [64, 128, 384], P('seq'), may hold values from -92 to 92
- suffix_values: bfloat16 [64, 128, 384], P('seq'), may hold values from -6 to 6
- group_of: int32 [64], replicated, may hold values from 0 to 7, as said below
- prefix_len: int32 [8], replicated, may hold values from 1 to 4096, as said below
- suffix_len: int32 [64], replicated, may hold values from 0 to 128, as said below
- mlp_gain: float32 [1152], replicated, may hold values from 0.1 to 1.9
- w_gate: bfloat16 [1152, 3072], P(None, 'tp'), may hold values from -0.1875 to 0.1875
- w_up: bfloat16 [1152, 3072], P(None, 'tp'), may hold values from -0.1875 to 0.1875
- w_down: bfloat16 [3072, 1152], P('tp'), may hold values from -0.109375 to 0.109375
Outputs:
- layer_out: bfloat16 [64, 1152], P('seq')
Inputs may be any that keep to these rules, and one draw needn't show every extreme that they name: `group_of`: prompt group of each request; every request reads its group's stored prefix. `prefix_len`: stored prefix positions in use for each group. `suffix_len`: stored suffix positions in use for each request.
All inputs are finite; a program needn't handle non-finite values.
Results may differ from a plain program's by a relative error of at most 0.018.
Values may be sent and summed in bfloat16 or wider, within the bound.
A program may use at most 192 MiB of HBM per device.

v0:
```python
import jax
import jax.numpy as jnp
from jax import lax
from jax.sharding import PartitionSpec as P

HEADS = 18
KV_HEADS = 6
HD = 64


NEG_FILL = -1e30


def rms_scale(values_in, gain_row):
    widened = values_in.astype(jnp.float32)
    factor = lax.rsqrt(jnp.mean(widened * widened, axis=-1, keepdims=True) + 1e-05)
    return (widened * factor * gain_row).astype(jnp.bfloat16)


def rotate_heads(blocks, position):
    half_dim = blocks.shape[-1] // 2
    frequency = jnp.power(10000.0, -jnp.arange(half_dim, dtype=jnp.float32) / half_dim)
    angles = position.astype(jnp.float32)[:, None, None] * frequency
    cosine = jnp.cos(angles)
    sine_part = jnp.sin(angles)
    low_half = blocks[..., :half_dim]
    high_half = blocks[..., half_dim:]
    return jnp.concatenate(
        [low_half * cosine - high_half * sine_part, high_half * cosine + low_half * sine_part],
        axis=-1,
    )


def slot_layout(device_tp, tp_count, slot_count):
    per_device = HEADS // tp_count
    surplus = HEADS % tp_count
    start_head = per_device * device_tp + jnp.minimum(device_tp, surplus)
    used_count = per_device + (device_tp < surplus).astype(jnp.int32)
    slot_ids = jnp.arange(slot_count, dtype=jnp.int32)
    head_ids = start_head + slot_ids
    slot_used = (slot_ids < used_count).astype(jnp.float32)
    kv_ids = jnp.minimum(head_ids, HEADS - 1) // (HEADS // KV_HEADS)
    return (kv_ids, slot_used)


def on_device(
    tokens,
    attn_gain,
    w_query,
    w_key,
    w_value,
    w_out,
    prefix_keys,
    prefix_values,
    suffix_keys,
    suffix_values,
    group_of,
    prefix_len,
    suffix_len,
    mlp_gain,
    w_gate,
    w_up,
    w_down,
):
    row_count = tokens.shape[0]
    slot_count = w_query.shape[1] // HD
    group_count = prefix_keys.shape[0]
    prefix_span = prefix_keys.shape[1]
    suffix_span = suffix_keys.shape[1]
    seq_index = lax.axis_index("seq")
    kv_ids, slot_used = slot_layout(lax.axis_index("tp"), lax.axis_size("tp"), slot_count)
    normed = rms_scale(tokens, attn_gain)
    queries = jnp.dot(normed, w_query, preferred_element_type=jnp.float32).reshape(
        row_count, slot_count, HD
    )
    new_keys = jnp.dot(normed, w_key, preferred_element_type=jnp.float32).reshape(
        row_count, KV_HEADS, HD
    )
    new_values = (
        jnp.dot(normed, w_value, preferred_element_type=jnp.float32)
        .astype(jnp.bfloat16)
        .reshape(row_count, KV_HEADS, HD)
    )
    own_start = seq_index * row_count
    own_groups = lax.dynamic_slice_in_dim(group_of, own_start, row_count)
    own_suffix = lax.dynamic_slice_in_dim(suffix_len, own_start, row_count)
    group_ids = jnp.arange(group_count, dtype=jnp.int32)
    own_prefix = jnp.sum(
        jnp.where(own_groups[:, None] == group_ids[None, :], prefix_len[None, :], 0), axis=1
    )
    position = own_prefix + own_suffix
    queries = rotate_heads(queries, position).astype(jnp.bfloat16)
    new_keys = rotate_heads(new_keys, position).astype(jnp.bfloat16)
    every_query = lax.all_gather(
        queries.reshape(row_count, slot_count * HD), "seq", axis=0, tiled=True
    )
    every_query = every_query.reshape(-1, slot_count, HD)
    request_count = every_query.shape[0]
    score_scale = HD ** (-0.5)
    pre_keys = jnp.take(prefix_keys.reshape(group_count, prefix_span, KV_HEADS, HD), kv_ids, axis=2)
    pre_values = jnp.take(
        prefix_values.reshape(group_count, prefix_span, KV_HEADS, HD), kv_ids, axis=2
    )
    pre_scores = (
        jnp.einsum("rsd,gpsd->rsgp", every_query, pre_keys, preferred_element_type=jnp.float32)
        * score_scale
    )
    pre_spots = seq_index * prefix_span + jnp.arange(prefix_span, dtype=jnp.int32)
    group_match = group_of[:, None] == group_ids[None, :]
    length_match = pre_spots[None, :] < prefix_len[:, None]
    pre_live = group_match[:, None, :, None] & length_match[None, None, :, :]
    top_score = jnp.max(
        jnp.where(pre_live, pre_scores, NEG_FILL).reshape(request_count, slot_count, -1), axis=2
    )
    pre_weights = jnp.where(pre_live, jnp.exp(pre_scores - top_score[:, :, None, None]), 0.0)
    totals = jnp.sum(pre_weights, axis=(2, 3))
    mixed_sum = jnp.einsum(
        "rsgp,gpsd->rsd",
        pre_weights.astype(jnp.bfloat16),
        pre_values,
        preferred_element_type=jnp.float32,
    )
    gathered = (
        lax.all_to_all(top_score[None], "seq", split_axis=1, concat_axis=0, tiled=True),
        lax.all_to_all(totals[None], "seq", split_axis=1, concat_axis=0, tiled=True),
        lax.all_to_all(mixed_sum[None], "seq", split_axis=1, concat_axis=0, tiled=True),
    )
    part_top = jnp.max(gathered[0], axis=0)
    part_scale = jnp.exp(gathered[0] - part_top[None])
    part_total = jnp.sum(part_scale * gathered[1], axis=0)
    part_mixed = jnp.sum(part_scale[..., None] * gathered[2], axis=0)
    suf_keys = jnp.take(suffix_keys.reshape(row_count, suffix_span, KV_HEADS, HD), kv_ids, axis=2)
    suf_values = jnp.take(
        suffix_values.reshape(row_count, suffix_span, KV_HEADS, HD), kv_ids, axis=2
    )
    suf_scores = (
        jnp.einsum("rsd,rjsd->rsj", queries, suf_keys, preferred_element_type=jnp.float32)
        * score_scale
    )
    suf_live = (jnp.arange(suffix_span, dtype=jnp.int32)[None, :] < own_suffix[:, None])[:, None, :]
    suf_top = jnp.max(jnp.where(suf_live, suf_scores, NEG_FILL), axis=2)
    own_keys = jnp.take(new_keys, kv_ids, axis=1).astype(jnp.float32)
    own_values = jnp.take(new_values, kv_ids, axis=1).astype(jnp.float32)
    own_score = jnp.sum(queries.astype(jnp.float32) * own_keys, axis=-1) * score_scale
    final_top = jnp.maximum(jnp.maximum(part_top, suf_top), own_score)
    carried = jnp.exp(part_top - final_top)
    suf_weights = jnp.where(suf_live, jnp.exp(suf_scores - final_top[:, :, None]), 0.0)
    own_weight = jnp.exp(own_score - final_top)
    denominator = carried * part_total + jnp.sum(suf_weights, axis=2) + own_weight
    own_low = lax.optimization_barrier(own_weight.astype(jnp.bfloat16)).astype(jnp.float32)
    numerator = carried[..., None] * part_mixed + own_low[..., None] * own_values
    numerator = numerator + jnp.einsum(
        "rsj,rjsd->rsd",
        suf_weights.astype(jnp.bfloat16),
        suf_values,
        preferred_element_type=jnp.float32,
    )
    attended = (numerator / denominator[..., None] * slot_used[None, :, None]).astype(jnp.bfloat16)
    head_part = jnp.dot(
        attended.reshape(row_count, slot_count * HD), w_out, preferred_element_type=jnp.float32
    )
    head_total = lax.psum(head_part.astype(jnp.bfloat16), "tp").astype(jnp.float32)
    hidden = (tokens.astype(jnp.float32) + head_total).astype(jnp.bfloat16)
    mlp_in = rms_scale(hidden, mlp_gain)
    gate_part = jnp.dot(mlp_in, w_gate, preferred_element_type=jnp.float32)
    up_part = jnp.dot(mlp_in, w_up, preferred_element_type=jnp.float32)
    activation = (jax.nn.silu(gate_part) * up_part).astype(jnp.bfloat16)
    down_part = jnp.dot(activation, w_down, preferred_element_type=jnp.float32)
    down_total = lax.psum(down_part.astype(jnp.bfloat16), "tp").astype(jnp.float32)
    return (hidden.astype(jnp.float32) + down_total).astype(jnp.bfloat16)


def solution(mesh):
    return jax.shard_map(
        on_device,
        mesh=mesh,
        in_specs=(
            P("seq", None),
            P(),
            P(None, "tp"),
            P(),
            P(),
            P("tp", None),
            P(None, "seq", None),
            P(None, "seq", None),
            P("seq", None, None),
            P("seq", None, None),
            P(),
            P(),
            P(),
            P(),
            P(None, "tp"),
            P(None, "tp"),
            P("tp", None),
        ),
        out_specs=P("seq", None),
        check_vma=False,
    )
```

profile of v0, /device:TPU:0, one launch (start us, length us, event | category | flops | bytes accessed | tf_op | source)
XLA Modules:
  0.0 168.3 jit_solution(12167891806951182724)
XLA Ops:
  4.5 1.4 fusion.64
  5.9 1.5 fusion.66
  10.7 32.4 %all_gather.3 = bf16[64,320]{1,0:T(8,128)(2,1)S(1)} all-gather(bf16[8,320]{1,0:T(8,128)(2,1)S(1)} %convert_element_type.88), channel_id=1, replica_groups=mesh['seq'=8,'tp'=4] {'seq'}, dimensions={0}, use_global_device_ids=true | all-gather | bytes 46080 | tf_op jit(solution)/shard_map/all_gather | solution.py:94
  43.3 4.7 %copy.79 = bf16[8,512,384]{1,2,0:T(8,128)(2,1)} copy(bf16[8,512,384]{2,1,0:T(8,128)(2,1)} %param.29) | data formatting | bytes 6291456 | tf_op args[6]
  47.9 3.9 %copy.80 = bf16[8,512,6,64]{1,3,0,2:T(8,128)(2,1)} copy(bf16[8,512,6,64]{1,3,2,0:T(8,128)(2,1)} %bitcast.92) | data formatting | bytes 6291456 | tf_op jit(solution)/shard_map/reshape | solution.py:100
  51.9 4.3 %gather_fusion = bf16[5,8,512,64]{2,3,1,0:T(8,128)(2,1)} fusion(bf16[8,512,6,64]{1,3,0,2:T(8,128)(2,1)} %copy.80, s32[1024]{0:T(1024)S(1)} %pad_clamp_fusion), kind=kCustom, calls=%fused_computation.clone | custom fusion | bytes 5242900 | tf_op jit(solution)/shard_map/jit(_take)/gather | solution.py:100
  56.3 3.2 %fusion = (f32[64,5]{0,1:T(8,128)S(1)}, f32[5,8,512,64]{2,3,1,0:T(8,128)S(1)}) fusion(pred[64,8,512]{2,0,1:T(8,128)(4,1)S(1)} %broadcast_and_fusion, bf16[64,5,64,1]{0,2,3,1:T(8,128)(2,1)S(1)} %bitcast.98, bf16[5,8,512,64]{2,3,1,0:T(8,128)(2,1)} %gather_fusion, pred[5]{0:T(512)(128)(4,1)S(1)} %get-tuple-element.36), kind=kOutput, calls=%fused_computation.8 | convolution fusion | flops 173014720 | bytes 8168709 | tf_op jit(solution)/shard_map/rsd,gpsd->rsgp/dot_general | solution.py:105
  62.6 5.4 %all-to-all-start.2 = ((f32[1,64,5]{2,0,1:T(1,128)}), f32[1,64,5]{2,0,1:T(1,128)}, u32[]{:S(2)}, u32[]{:S(2)}) async-start(f32[1,64,5]{2,0,1:T(1,128)} %copy.97), calls=%async_computation.2 | async-start | bytes 65536 | tf_op jit(solution)/shard_map/all_to_all | solution.py:125
  68.9 1.5 copy.88
  71.1 2.3 %copy.96 = bf16[8,128,384]{1,2,0:T(8,128)(2,1)} copy(bf16[8,128,384]{2,1,0:T(8,128)(2,1)} %param.32) | data formatting | bytes 1572864 | tf_op args[9]
  73.4 1.8 %gather_fusion.5 = bf16[5,8,128,64]{2,3,1,0:T(8,128)(2,1)S(1)} fusion(bf16[8,128,6,64]{1,3,2,0:T(8,128)(2,1)} %bitcast.95, s32[1024]{0:T(1024)S(1)} %pad_clamp_fusion), kind=kCustom, calls=%fused_computation.4.clone | custom fusion | bytes 1310740 | tf_op jit(solution)/shard_map/jit(_take)/gather | solution.py:133
  75.2 4.7 %copy.91 = bf16[8,512,384]{1,2,0:T(8,128)(2,1)} copy(bf16[8,512,384]{2,1,0:T(8,128)(2,1)} %param.30) | data formatting | bytes 6291456 | tf_op args[7]
  79.9 3.9 %copy.92 = bf16[8,512,6,64]{1,3,0,2:T(8,128)(2,1)} copy(bf16[8,512,6,64]{1,3,2,0:T(8,128)(2,1)} %bitcast.93) | data formatting | bytes 6291456 | tf_op jit(solution)/shard_map/reshape | solution.py:102
  83.8 4.3 %gather_fusion.3 = bf16[5,8,512,64]{2,3,1,0:T(8,128)(2,1)} fusion(bf16[8,512,6,64]{1,3,0,2:T(8,128)(2,1)} %copy.92, s32[1024]{0:T(1024)S(1)} %pad_clamp_fusion), kind=kCustom, calls=%fused_computation.3.clone | custom fusion | bytes 5242900 | tf_op jit(solution)/shard_map/jit(_take)/gather | solution.py:101
  88.2 5.6 %fusion.20 = f32[1,64,5,64]{1,3,2,0:T(8,128)} fusion(f32[5,8,512,64]{2,3,1,0:T(8,128)} %copy-done.1, f32[64,5]{0,1:T(8,128)S(1)} %get-tuple-element.34, pred[64,8,512]{2,0,1:T(8,128)(4,1)S(1)} %broadcast_and_fusion, bf16[5,8,512,64]{2,3,1,0:T(8,128)(2,1)} %gather_fusion.3, pred[5]{0:T(512)(128)(4,1)S(1)} %get-tuple-element.36), kind=kOutput, calls=%fused_computation.29 | convolution fusion | flops 174325760 | bytes 8209669 | tf_op jit(solution)/shard_map/rsgp,gpsd->rsd/dot_general | solution.py:117
  96.4 6.0 %all-to-all-start = ((f32[1,64,5]{2,0,1:T(1,128)}), f32[1,64,5]{2,0,1:T(1,128)}, u32[]{:S(2)}, u32[]{:S(2)}) async-start(f32[1,64,5]{2,0,1:T(1,128)} %copy.86), calls=%async_computation | async-start | bytes 65536 | tf_op jit(solution)/shard_map/all_to_all | solution.py:124
  102.4 1.4 select_reduce_fusion
  105.2 1.4 gather_fusion.4
  106.6 1.7 %copy.93 = f32[1,64,5,64]{3,0,2,1:T(1,128)} copy(f32[1,64,5,64]{1,3,2,0:T(8,128)} %fusion.20) | data formatting | bytes 163840 | tf_op jit(solution)/shard_map/broadcast_in_dim | solution.py:126
  108.9 2.7 %reduce.1 = f32[64,5,64]{2,1,0:T(8,128)} reduce(f32[64,5,1,64]{3,2,1,0:T(1,128)} %bitcast.96, f32[]{:T(128)} %broadcast.335), dimensions={2}, to_apply=%bitcast.79.reduce_sub_computation | reduce | bytes 163844
  111.5 1.7 %reshape.341 = f32[8,1,2560]{2,1,0:T(1,128)} reshape(f32[64,5,64]{2,1,0:T(8,128)} %reduce.1) | data formatting | bytes 163840
  113.3 1.5 copy.111
  114.7 6.0 %all-to-all-start.1 = ((f32[8,1,2560]{2,1,0:T(1,128)}), f32[8,1,2560]{2,1,0:T(1,128)}, u32[]{:S(2)}, u32[]{:S(2)}) async-start(f32[8,1,2560]{2,1,0:T(1,128)} %reshape.341), calls=%async_computation.1 | async-start | bytes 163840 | tf_op jit(solution)/shard_map/all_to_all | solution.py:126
  120.7 1.5 copy.110
  127.9 2.1 %fusion.26 = f32[8,5,1,64]{3,2,1,0:T(1,128)} fusion(bf16[8,128,5,64]{1,3,0,2:T(8,128)(2,1)} %get-tuple-element.33, bf16[8,5,128,1]{2,0,1,3:T(8,128)(2,1)S(1)} %get-tuple-element.29), kind=kOutput, calls=%fused_computation.33 | convolution fusion | flops 655360 | bytes 675840 | tf_op jit(solution)/shard_map/rsj,rjsd->rsd/dot_general | solution.py:152
  131.3 2.3 %reduce.2 = f32[8,2560]{1,0:T(8,128)} reduce(f32[8,1,2560]{2,1,0:T(1,128)} %all-to-all-done.1, f32[]{:T(128)} %broadcast.335), dimensions={1}, to_apply=%all_to_all.14.reduce_sub_computation | reduce | bytes 163844 | tf_op jit(solution)/shard_map/all_to_all | solution.py:126
  133.7 1.7 %reshape.342 = f32[64,5,1,64]{3,2,1,0:T(1,128)} reshape(f32[8,2560]{1,0:T(8,128)} %reduce.2) | data formatting | bytes 163840
  138.0 2.0 %convolution_convert_fusion.1 = bf16[8,1152]{1,0:T(8,128)(2,1)} fusion(bf16[8,320]{1,0:T(8,128)(2,1)} %reshape.268, bf16[320,1152]{1,0:T(8,128)(2,1)} %param.28), kind=kOutput, calls=%fused_computation.26 | convolution fusion | flops 5907456 | bytes 760832 | tf_op jit(solution)/shard_map/dot_general | solution.py:159
  139.9 11.4 %psum.14 = bf16[8,1152]{1,0:T(8,128)(2,1)} all-reduce(bf16[8,1152]{1,0:T(8,128)(2,1)} %convolution_convert_fusion.1), channel_id=1, replica_groups=mesh['seq'=8,'tp'=4] {'tp'}, use_global_device_ids=true, to_apply=%region_10.14 | all-reduce | flops 9216 | bytes 36864 | tf_op jit(solution)/shard_map/psum | solution.py:162
  152.8 1.7 fusion.56
  154.5 2.2 %convolution_convert_fusion = bf16[8,1152]{1,0:T(8,128)(2,1)S(1)} fusion(bf16[768,1152]{1,0:T(8,128)(2,1)S(1)} %copy-done, bf16[1152,768]{1,0:T(8,128)(2,1)} %param.38, f32[8,768]{1,0:T(8,128)} %fusion.56, bf16[8,1152]{1,0:T(8,128)(2,1)} %copy-done.5, f32[1152]{0:T(1024)S(1)} %copy-done.8, f32[8]{0:T(128)S(1)} %add_rsqrt_fusion), kind=kOutput, calls=%fused_computation.25 | convolution fusion | flops 28394496 | bytes 3605024 | tf_op jit(solution)/shard_map/dot_general | solution.py:168
  156.7 11.0 %psum.15 = bf16[8,1152]{1,0:T(8,128)(2,1)S(1)} all-reduce(bf16[8,1152]{1,0:T(8,128)(2,1)S(1)} %convolution_convert_fusion), channel_id=1, replica_groups=mesh['seq'=8,'tp'=4] {'tp'}, use_global_device_ids=true, to_apply=%region_12.16 | all-reduce | flops 9216 | bytes 36864 | tf_op jit(solution)/shard_map/psum | solution.py:169
  (80 shorter events, 28.8 us)
Async XLA Ops:
  0.0 154.5 %copy-start = (bf16[768,1152]{1,0:T(8,128)(2,1)S(1)}, bf16[768,1152]{1,0:T(8,128)(2,1)}, u32[]{:S(2)}) copy-start(bf16[768,1152]{1,0:T(8,128)(2,1)} %param.39) | copy-start | bytes 5308420
  2.9 90.8 %copy-start.10 = (pred[5]{0:T(512)(128)(4,1)}, pred[5]{0:T(512)(128)(4,1)S(1)}, u32[]{:S(2)}) copy-start(pred[5]{0:T(512)(128)(4,1)S(1)} %get-tuple-element.36) | copy-start | bytes 19
  4.5 79.4 %copy-start.9 = (s32[1024]{0:T(1024)}, s32[1024]{0:T(1024)S(1)}, u32[]{:S(2)}) copy-start(s32[1024]{0:T(1024)S(1)} %pad_clamp_fusion) | copy-start | bytes 12292
  59.6 2.3 %copy-start.1 = (f32[5,8,512,64]{2,3,1,0:T(8,128)}, f32[5,8,512,64]{2,3,1,0:T(8,128)S(1)}, u32[]{:S(2)}) copy-start(f32[5,8,512,64]{2,3,1,0:T(8,128)S(1)} %get-tuple-element.35) | copy-start | bytes 15728644
  59.6 8.4 %copy-start.3 = (bf16[1152,384]{1,0:T(8,128)(2,1)S(1)}, bf16[1152,384]{1,0:T(8,128)(2,1)}, u32[]{:S(2)}) copy-start(bf16[1152,384]{1,0:T(8,128)(2,1)} %param.27) | copy-start | bytes 2654212
  59.6 8.4 %copy-start.4 = (bf16[8,1152]{1,0:T(8,128)(2,1)S(1)}, bf16[8,1152]{1,0:T(8,128)(2,1)}, u32[]{:S(2)}) copy-start(bf16[8,1152]{1,0:T(8,128)(2,1)} %param.23) | copy-start | bytes 55300
  59.6 8.4 %copy-start.7 = (f32[1152]{0:T(1024)S(1)}, f32[1152]{0:T(1024)}, u32[]{:S(2)}) copy-start(f32[1152]{0:T(1024)} %param.24) | copy-start | bytes 13828
  62.6 33.8 %all-to-all-start.2 = ((f32[1,64,5]{2,0,1:T(1,128)}), f32[1,64,5]{2,0,1:T(1,128)}, u32[]{:S(2)}, u32[]{:S(2)}) async-start(f32[1,64,5]{2,0,1:T(1,128)} %copy.97), calls=%async_computation.2 | async-start | bytes 65536 | tf_op jit(solution)/shard_map/all_to_all | solution.py:125
  93.7 1.9 %copy-start.12 = (s32[8]{0:T(128)S(1)}, s32[8]{0:T(128)}, u32[]{:S(2)}) copy-start(s32[8]{0:T(128)} %get-tuple-element.19) | copy-start | bytes 100
  94.8 58.0 %copy-start.2 = (bf16[1152,768]{1,0:T(8,128)(2,1)S(1)}, bf16[1152,768]{1,0:T(8,128)(2,1)}, u32[]{:S(2)}) copy-start(bf16[1152,768]{1,0:T(8,128)(2,1)} %param.37) | copy-start | bytes 5308420
  95.7 6.7 %copy-start.11 = (pred[8,128]{1,0:T(8,128)(4,1)}, pred[8,128]{1,0:T(8,128)(4,1)S(1)}, u32[]{:S(2)}) copy-start(pred[8,128]{1,0:T(8,128)(4,1)S(1)} %iota_compare_fusion) | copy-start | bytes 3076
  96.4 18.3 %all-to-all-start = ((f32[1,64,5]{2,0,1:T(1,128)}), f32[1,64,5]{2,0,1:T(1,128)}, u32[]{:S(2)}, u32[]{:S(2)}) async-start(f32[1,64,5]{2,0,1:T(1,128)} %copy.86), calls=%async_computation | async-start | bytes 65536 | tf_op jit(solution)/shard_map/all_to_all | solution.py:124
  114.7 16.6 %all-to-all-start.1 = ((f32[8,1,2560]{2,1,0:T(1,128)}), f32[8,1,2560]{2,1,0:T(1,128)}, u32[]{:S(2)}, u32[]{:S(2)}) async-start(f32[8,1,2560]{2,1,0:T(1,128)} %reshape.341), calls=%async_computation.1 | async-start | bytes 163840 | tf_op jit(solution)/shard_map/all_to_all | solution.py:126
  138.0 16.5 %copy-start.8 = (f32[1152]{0:T(1024)S(1)}, f32[1152]{0:T(1024)}, u32[]{:S(2)}) copy-start(f32[1152]{0:T(1024)} %param.36) | copy-start | bytes 13828
  152.2 0.6 copy-start.5
  154.5 13.3 %copy-start.6 = (bf16[8,1152]{1,0:T(8,128)(2,1)S(1)}, bf16[8,1152]{1,0:T(8,128)(2,1)}, u32[]{:S(2)}) copy-start(bf16[8,1152]{1,0:T(8,128)(2,1)} %copy-done.5) | copy-start | bytes 55300
where the time goes:
time: 170 us; the launch traced here: 168 us
  blocking collectives  54.8 us (32%)
  local copies, waits for them, and re-layouts  49.8 us (29%)
  other arithmetic  24.6 us (14%)
  matrix products  21.5 us (13%)
  starting transfers between devices  17.4 us (10%)
    all_gather x1, blocking collectives, on_device(): lax.all_gather(queries.reshape(row_count, slot_count * HD), 'seq', axis=0...  32.4 us
    unnamed x34, local copies, waits for them, and re-layouts  19.6 us
    psum x1, blocking collectives, on_device(): lax.psum(head_part.astype(jnp.bfloat16), 'tp').astype(jnp.float32)  11.4 us
    psum x1, blocking collectives, on_device(): lax.psum(down_part.astype(jnp.bfloat16), 'tp').astype(jnp.float32)  11 us
    all_to_all x1, starting transfers between devices, on_device(): lax.all_to_all(mixed_sum[None], 'seq', split_axis=1, concat_axis=0, tiled...  5.99 us
    all_to_all x1, starting transfers between devices, on_device(): lax.all_to_all(top_score[None], 'seq', split_axis=1, concat_axis=0, tiled...  5.99 us
    dot_general x1, matrix products, on_device(): jnp.einsum('rsgp,gpsd->rsd', pre_weights.astype(jnp.bfloat16), pre_values...  5.57 us
    all_to_all x1, starting transfers between devices, on_device(): lax.all_to_all(totals[None], 'seq', split_axis=1, concat_axis=0, tiled=True)  5.41 us
  transfers between devices with their start and end apart: 3, of which 0 were waited for; matrix products, arithmetic and copies ran while one was open for 30% of the time, Pallas kernels for 0%

commit v1 on v0

v1 whole, which is shorter than its diff:
```python
import functools

import jax
import jax.numpy as jnp
from jax import lax
from jax.experimental import pallas as pl
from jax.experimental.pallas import tpu as pltpu
from jax.sharding import PartitionSpec as P

HEADS = 18
KV_HEADS = 6
HD = 64
NEG = -1e30
WIDE = 256
PACK = 384
MESH = pl.DeviceIdType.MESH
F32 = jnp.float32
BF16 = jnp.bfloat16


def lane_ids(shape):
    return lax.broadcasted_iota(jnp.int32, shape, len(shape) - 1)


def rms(values, gain):
    wide = values.astype(F32)
    factor = lax.rsqrt(jnp.mean(wide * wide, axis=-1, keepdims=True) + 1e-05)
    return (wide * factor * gain).astype(BF16)


def dot(a, b):
    return jnp.dot(a, b, preferred_element_type=F32)


def dot_t(a, b):
    return lax.dot_general(a, b, (((1,), (1,)), ((), ())), preferred_element_type=F32)


def rotate(x, cosine, sine):
    width = x.shape[-1]
    low = lane_ids(x.shape) % HD < HD // 2
    ahead = pltpu.roll(x, width - HD // 2, 1)
    behind = pltpu.roll(x, HD // 2, 1)
    return x * cosine + jnp.where(low, -ahead, behind) * sine


def spread(q, local_kv):
    rows = q.shape[0]
    half = lane_ids((rows, 128)) < HD
    quarter = lane_ids((rows, WIDE)) // HD
    blocks = []
    for s, kv in enumerate(local_kv):
        pair = q[:, 128 * (s // 2) : 128 * (s // 2) + 128]
        turned = pltpu.roll(pair, HD, 1)
        both = jnp.where(half, pair, turned) if s % 2 == 0 else jnp.where(half, turned, pair)
        wide = jnp.concatenate([both, both], axis=1)
        blocks.append(jnp.where(quarter == kv, wide, 0.0))
    return jnp.concatenate(blocks, axis=0)


def pack(mixed, tops, totals, local_kv, rows):
    lanes = lane_ids((rows, 128))
    quarter = lane_ids((rows, WIDE)) // HD
    both = []
    for s, kv in enumerate(local_kv):
        part = jnp.where(quarter == kv, mixed[s * rows : (s + 1) * rows], 0.0)
        part = part[:, :128] + part[:, 128:]
        both.append(part + pltpu.roll(part, HD, 1))
    last = both[4]
    for s in range(5):
        top = tops[s * rows : (s + 1) * rows]
        total = totals[s * rows : (s + 1) * rows]
        last = jnp.where(lanes == HD + s, top, last)
        last = jnp.where(lanes == HD + 8 + s, total, last)
    return jnp.concatenate(
        [
            jnp.where(lanes < HD, both[0], both[1]),
            jnp.where(lanes < HD, both[2], both[3]),
            jnp.where((lanes < HD) | (lanes < HD + 16), last, 0.0),
        ],
        axis=1,
    )


def column(ref, start, rows):
    ids = lax.broadcasted_iota(jnp.int32, (8, 1), 0)
    blocks = []
    for block in range(rows // 8):
        col = jnp.zeros((8, 1), jnp.int32)
        for r in range(8):
            col = jnp.where(ids == r, ref[start + block * 8 + r], col)
        blocks.append(col)
    return blocks[0] if len(blocks) == 1 else jnp.concatenate(blocks, axis=0)


def kernel(
    n_seq,
    n_tp,
    tokens_h,
    attn_gain_h,
    w_query_h,
    w_key_h,
    w_value_h,
    w_out_h,
    prefix_keys_h,
    prefix_values_h,
    suffix_keys_h,
    suffix_values_h,
    group_of,
    prefix_len,
    suffix_len,
    mlp_gain_h,
    w_gate_h,
    w_up_h,
    w_down_h,
    out_ref,
    tokens,
    attn_gain,
    w_query,
    w_key,
    w_value,
    w_out,
    keys,
    values,
    suf_keys,
    suf_values,
    mlp_gain,
    w_gate,
    w_up,
    w_down,
    queries,
    send_parts,
    parts,
    head_parts,
    down_parts,
    local_sem,
    group_sem,
    q_send,
    q_recv,
    p_send,
    p_recv,
    h_send,
    h_recv,
    d_send,
    d_recv,
):
    seq = lax.axis_index("seq")
    tp = lax.axis_index("tp")
    rows = tokens.shape[0]
    groups, span = keys.shape[0], keys.shape[1]
    suffix_span = suf_keys.shape[1]

    barrier = pltpu.get_barrier_semaphore()

    def greet(k, carry):
        pl.semaphore_signal(
            barrier, inc=1, device_id={"seq": lax.rem(seq + k, n_seq)}, device_id_type=MESH
        )
        return carry

    if n_seq <= 8:
        for k in range(1, n_seq):
            greet(k, 0)
    else:
        lax.fori_loop(1, n_seq, greet, 0)
    for k in range(1, n_tp):
        pl.semaphore_signal(
            barrier, inc=1, device_id={"tp": lax.rem(tp + k, n_tp)}, device_id_type=MESH
        )

    per, surplus = HEADS // n_tp, HEADS % n_tp
    first_head = per * tp + jnp.minimum(tp, surplus)
    used = per + (tp < surplus).astype(jnp.int32)
    share = HEADS // KV_HEADS
    first_block = jnp.minimum((first_head // share) // 2, 1)
    local_kv = [
        jnp.minimum(first_head + s, HEADS - 1) // share - 2 * first_block for s in range(5)
    ]
    columns = pl.ds(pl.multiple_of(first_block * 128, 128), WIDE)

    copies = {}
    for i, (name, src, dst) in enumerate(
        [
            ("tokens", tokens_h, tokens),
            ("attn_gain", attn_gain_h, attn_gain),
            ("w_query", w_query_h, w_query),
            ("w_key", w_key_h.at[:, columns], w_key),
            ("w_value", w_value_h.at[:, columns], w_value),
            ("suf_keys", suffix_keys_h.at[:, :, columns], suf_keys),
            ("suf_values", suffix_values_h.at[:, :, columns], suf_values),
            ("w_out", w_out_h, w_out),
            ("mlp_gain", mlp_gain_h, mlp_gain),
            ("w_gate", w_gate_h, w_gate),
            ("w_up", w_up_h, w_up),
            ("w_down", w_down_h, w_down),
        ]
    ):
        copies[name] = pltpu.make_async_copy(src, dst, local_sem.at[i])
    key_copies = [
        pltpu.make_async_copy(prefix_keys_h.at[g, :, columns], keys.at[g], group_sem.at[0, g])
        for g in range(groups)
    ]
    value_copies = [
        pltpu.make_async_copy(prefix_values_h.at[g, :, columns], values.at[g], group_sem.at[1, g])
        for g in range(groups)
    ]
    for name in ("tokens", "attn_gain", "w_query", "w_key", "w_value", "suf_keys", "suf_values"):
        copies[name].start()
    for g in range(groups):
        key_copies[g].start()
        value_copies[g].start()
    for name in ("w_out", "mlp_gain", "w_gate", "w_up", "w_down"):
        copies[name].start()

    own_start = seq * rows
    own_group = column(group_of, own_start, rows)
    own_suffix = column(suffix_len, own_start, rows)
    own_prefix = jnp.zeros((rows, 1), jnp.int32)
    for g in range(groups):
        own_prefix = jnp.where(own_group == g, prefix_len[g], own_prefix)
    position = (own_prefix + own_suffix).astype(F32)
    turn = lane_ids((rows, 128)) % (HD // 2)
    frequency = jnp.ones((rows, 128), F32)
    for bit in range(5):
        step = 10000.0 ** (-(2**bit) / 32.0)
        frequency = jnp.where((turn // 2**bit) % 2 == 1, frequency * step, frequency)
    angles = position * frequency
    cosine, sine = jnp.cos(angles), jnp.sin(angles)
    cos2 = jnp.concatenate([cosine, cosine], axis=1)
    sin2 = jnp.concatenate([sine, sine], axis=1)
    cos3 = jnp.concatenate([cos2, cosine], axis=1)
    sin3 = jnp.concatenate([sin2, sine], axis=1)

    copies["tokens"].wait()
    copies["attn_gain"].wait()
    normed = rms(tokens[...], attn_gain[...])
    copies["w_query"].wait()
    q = dot(normed, w_query[...])
    q = jnp.concatenate([q, jnp.zeros((rows, PACK - q.shape[1]), F32)], axis=1)
    q_own = rotate(q, cos3, sin3).astype(BF16)
    queries[seq] = q_own
    pl.semaphore_wait(barrier, n_seq - 1 + n_tp - 1)

    def seq_copy(src, dst, send, recv, k):
        return pltpu.make_async_remote_copy(
            src_ref=src,
            dst_ref=dst,
            send_sem=send.at[k],
            recv_sem=recv.at[seq],
            device_id={"seq": lax.rem(seq + k, n_seq)},
            device_id_type=MESH,
        )

    def seq_wait(buf, send, recv, k):
        other = lax.rem(seq + k, n_seq)
        return pltpu.make_async_remote_copy(
            src_ref=buf.at[other],
            dst_ref=buf.at[other],
            send_sem=send.at[k],
            recv_sem=recv.at[other],
            device_id={"seq": other},
            device_id_type=MESH,
        )

    def over_peers(act):
        if n_seq <= 8:
            for k in range(1, n_seq):
                act(k)
        else:

            def step(k, carry):
                act(k)
                return carry

            lax.fori_loop(1, n_seq, step, 0)

    over_peers(
        lambda k: seq_copy(queries.at[seq], queries.at[seq], q_send, q_recv, k).start()
    )

    copies["w_key"].wait()
    copies["w_value"].wait()
    new_keys = rotate(dot(normed, w_key[...]), cos2, sin2).astype(BF16).astype(F32)
    new_values = dot(normed, w_value[...]).astype(BF16).astype(F32)
    q_wide = spread(q_own.astype(F32) * HD ** (-0.5), local_kv)
    own_score = jnp.sum(q_wide * jnp.concatenate([new_keys] * 5, axis=0), axis=1, keepdims=True)
    copies["suf_keys"].wait()
    suf_all = suf_keys[...].reshape(rows * suffix_span, WIDE)
    suf_scores = dot_t(q_wide.astype(BF16), suf_all)
    shape = suf_scores.shape
    spot = lane_ids(shape)
    row_id = lax.broadcasted_iota(jnp.int32, shape, 0) % rows
    limit = jnp.concatenate([own_suffix] * 5, axis=0)
    suf_live = (spot >= row_id * suffix_span) & (spot < row_id * suffix_span + limit)
    suf_scores = jnp.where(suf_live, suf_scores, NEG)
    suf_top = jnp.maximum(jnp.max(suf_scores, axis=1, keepdims=True), own_score)
    suf_weights = jnp.exp(suf_scores - suf_top)
    own_weight = jnp.exp(own_score - suf_top)
    suf_total = jnp.sum(suf_weights, axis=1, keepdims=True) + own_weight
    copies["suf_values"].wait()
    suf_mixed = dot(suf_weights.astype(BF16), suf_values[...].reshape(rows * suffix_span, WIDE))
    own_low = own_weight.astype(BF16).astype(F32)
    suf_mixed = suf_mixed + own_low * jnp.concatenate([new_values] * 5, axis=0)
    suf_part = pack(suf_mixed, suf_top, suf_total, local_kv, rows)

    over_peers(lambda k: seq_wait(queries, q_send, q_recv, k).wait_recv())
    for g in range(groups):
        key_copies[g].wait()
        value_copies[g].wait()

    per_chunk = min(8, n_seq)
    chunk_rows = per_chunk * rows
    spots = seq * span + lane_ids((1, span))

    def prefix_chunk(c, carry):
        q_all = queries[pl.ds(c * per_chunk, per_chunk)].astype(F32).reshape(chunk_rows, PACK)
        q_all = spread(q_all * HD ** (-0.5), local_kv).astype(BF16)
        group = column(group_of, c * chunk_rows, chunk_rows)
        group = jnp.concatenate([group] * 5, axis=0)
        mixed = jnp.zeros((5 * chunk_rows, WIDE), F32)
        tops = jnp.full((5 * chunk_rows, 1), NEG, F32)
        totals = jnp.zeros((5 * chunk_rows, 1), F32)
        for g in range(groups):
            scores = jnp.where(spots < prefix_len[g], dot_t(q_all, keys[g]), NEG)
            top = jnp.max(scores, axis=1, keepdims=True)
            member = group == g
            tops = jnp.where(member, top, tops)
            weights = jnp.exp(scores - jnp.where(member, top, -NEG))
            totals += jnp.sum(weights, axis=1, keepdims=True)
            mixed += dot(weights.astype(BF16), values[g])
        packed = pack(mixed, tops, totals, local_kv, chunk_rows)
        send_parts[pl.ds(c * per_chunk, per_chunk)] = packed.reshape(per_chunk, rows, PACK)
        return carry

    if n_seq == per_chunk:
        prefix_chunk(0, 0)
    else:
        lax.fori_loop(0, n_seq // per_chunk, prefix_chunk, 0)

    def send_part(k):
        other = lax.rem(seq + k, n_seq)
        seq_copy(send_parts.at[other], parts.at[seq], p_send, p_recv, k).start()

    over_peers(send_part)
    parts[seq] = send_parts[seq]
    over_peers(lambda k: seq_wait(parts, p_send, p_recv, k).wait_recv())

    every = parts[...]
    ends = every[:, :, 256:]
    suf_end = suf_part[:, 256:]
    top = jnp.maximum(jnp.max(ends, axis=0), suf_end)
    scales = jnp.exp(ends - top[None])
    suf_scale = jnp.exp(suf_end - top)
    total = suf_scale * pltpu.roll(suf_end, 120, 1)
    for i in range(n_seq):
        total = total + scales[i] * pltpu.roll(ends[i], 120, 1)
    used_lane = lane_ids((rows, 128)) - HD < used
    share_of = jnp.where(used_lane, 1.0 / total, 0.0)
    half = lane_ids((rows, 128)) < HD

    def weigh(scale, part):
        scale = scale * share_of
        cols = [scale[:, HD + s : HD + s + 1] for s in range(5)]
        return jnp.concatenate(
            [
                jnp.where(half, cols[0], cols[1]) * part[:, :128],
                jnp.where(half, cols[2], cols[3]) * part[:, 128:256],
                jnp.where(half, cols[4], 0.0) * part[:, 256:],
            ],
            axis=1,
        )

    attended = weigh(suf_scale, suf_part)
    for i in range(n_seq):
        attended = attended + weigh(scales[i], every[i])
    attended = attended[:, : 5 * HD].astype(BF16)

    def tp_sum(buf, send, recv):
        for k in range(1, n_tp):
            pltpu.make_async_remote_copy(
                src_ref=buf.at[tp],
                dst_ref=buf.at[tp],
                send_sem=send.at[k],
                recv_sem=recv.at[tp],
                device_id={"tp": lax.rem(tp + k, n_tp)},
                device_id_type=MESH,
            ).start()
        for k in range(1, n_tp):
            other = lax.rem(tp + k, n_tp)
            pltpu.make_async_remote_copy(
                src_ref=buf.at[other],
                dst_ref=buf.at[other],
                send_sem=send.at[k],
                recv_sem=recv.at[other],
                device_id={"tp": other},
                device_id_type=MESH,
            ).wait_recv()
        total = buf[0].astype(F32)
        for i in range(1, n_tp):
            total = total + buf[i].astype(F32)
        return total

    copies["w_out"].wait()
    head_parts[tp] = dot(attended, w_out[...]).astype(BF16)
    hidden = (tokens[...].astype(F32) + tp_sum(head_parts, h_send, h_recv)).astype(BF16)
    copies["mlp_gain"].wait()
    mlp_in = rms(hidden, mlp_gain[...])
    copies["w_gate"].wait()
    gate = dot(mlp_in, w_gate[...])
    copies["w_up"].wait()
    up = dot(mlp_in, w_up[...])
    activation = (gate / (1.0 + jnp.exp(-gate)) * up).astype(BF16)
    copies["w_down"].wait()
    down_parts[tp] = dot(activation, w_down[...]).astype(BF16)
    total = tp_sum(down_parts, d_send, d_recv)
    out_ref[...] = (hidden.astype(F32) + total).astype(BF16)

    over_peers(
        lambda k: seq_copy(queries.at[seq], queries.at[seq], q_send, q_recv, k).wait_send()
    )

    def sent_part(k):
        other = lax.rem(seq + k, n_seq)
        seq_copy(send_parts.at[other], parts.at[seq], p_send, p_recv, k).wait_send()

    over_peers(sent_part)
    for buf, send, recv in ((head_parts, h_send, h_recv), (down_parts, d_send, d_recv)):
        for k in range(1, n_tp):
            pltpu.make_async_remote_copy(
                src_ref=buf.at[tp],
                dst_ref=buf.at[tp],
                send_sem=send.at[k],
                recv_sem=recv.at[tp],
                device_id={"tp": lax.rem(tp + k, n_tp)},
                device_id_type=MESH,
            ).wait_send()


def on_device(n_seq, n_tp, *args):
    tokens, w_query, w_out, w_gate, w_down = args[0], args[2], args[5], args[14], args[16]
    prefix, suffix = args[6], args[8]
    rows, width = tokens.shape
    groups, span, _ = prefix.shape
    hidden_units = w_gate.shape[1]
    dma = pltpu.SemaphoreType.DMA
    args = list(args)
    args[1] = args[1].reshape(1, width)
    args[13] = args[13].reshape(1, width)
    in_specs = [pl.BlockSpec(memory_space=pl.ANY)] * len(args)
    for i in (10, 11, 12):
        in_specs[i] = pl.BlockSpec(memory_space=pltpu.SMEM)
    return pl.pallas_call(
        functools.partial(kernel, n_seq, n_tp),
        out_shape=jax.ShapeDtypeStruct((rows, width), BF16),
        in_specs=in_specs,
        out_specs=pl.BlockSpec(memory_space=pltpu.VMEM),
        scratch_shapes=[
            pltpu.VMEM((rows, width), BF16),
            pltpu.VMEM((1, width), F32),
            pltpu.VMEM(w_query.shape, BF16),
            pltpu.VMEM((width, WIDE), BF16),
            pltpu.VMEM((width, WIDE), BF16),
            pltpu.VMEM(w_out.shape, BF16),
            pltpu.VMEM((groups, span, WIDE), BF16),
            pltpu.VMEM((groups, span, WIDE), BF16),
            pltpu.VMEM((rows, suffix.shape[1], WIDE), BF16),
            pltpu.VMEM((rows, suffix.shape[1], WIDE), BF16),
            pltpu.VMEM((1, width), F32),
            pltpu.VMEM(w_gate.shape, BF16),
            pltpu.VMEM(w_gate.shape, BF16),
            pltpu.VMEM(w_down.shape, BF16),
            pltpu.VMEM((n_seq, rows, PACK), BF16),
            pltpu.VMEM((n_seq, rows, PACK), F32),
            pltpu.VMEM((n_seq, rows, PACK), F32),
            pltpu.VMEM((n_tp, rows, width), BF16),
            pltpu.VMEM((n_tp, rows, width), BF16),
            dma((12,)),
            dma((2, groups)),
            dma((n_seq,)),
            dma((n_seq,)),
            dma((n_seq,)),
            dma((n_seq,)),
            dma((n_tp,)),
            dma((n_tp,)),
            dma((n_tp,)),
            dma((n_tp,)),
        ],
        compiler_params=pltpu.CompilerParams(
            collective_id=0, has_side_effects=True, vmem_limit_bytes=56 * 1024 * 1024
        ),
    )(*args)


def solution(mesh):
    return jax.shard_map(
        functools.partial(on_device, mesh.shape["seq"], mesh.shape["tp"]),
        mesh=mesh,
        in_specs=(
            P("seq", None),
            P(),
            P(None, "tp"),
            P(),
            P(),
            P("tp", None),
            P(None, "seq", None),
            P(None, "seq", None),
            P("seq", None, None),
            P("seq", None, None),
            P(),
            P(),
            P(),
            P(),
            P(None, "tp"),
            P(None, "tp"),
            P("tp", None),
        ),
        out_specs=P("seq", None),
        check_vma=False,
    )
```

time: 170 us -> 32.6 us (0.19)
  blocking collectives: 54.8 us -> 0 us
  local copies, waits for them, and re-layouts: 49.8 us -> 6.09 us
  Pallas kernels: 0 us -> 26.2 us
  other arithmetic: 24.6 us -> 0 us
  matrix products: 21.5 us -> 0 us
  starting transfers between devices: 17.4 us -> 0 us
    all_gather x1 -> x0, blocking collectives: 32.4 us -> none  [on_device(): lax.all_gather(queries.reshape(row_count, slot_count * HD), 'seq', axis=0...]
    pallas_call x0 -> x1, Pallas kernels: none -> 26.2 us  [on_device(): pl.pallas_call(functools.partial(kernel, n_seq, n_tp), out_shape=jax.Shap...]
    psum x2 -> x0, blocking collectives: 22.4 us -> none  [the longest x1 11.4 us: on_device(): lax.psum(head_part.astype(jnp.bfloat16), 'tp').astype(jnp.float32)]
    dot_general x10 -> x0, matrix products: 21.5 us -> none  [the longest x1 5.57 us: on_device(): jnp.einsum('rsgp,gpsd->rsd', pre_weights.astype(jnp.bfloat16), pre_values...]
    all_to_all x3 -> x0, starting transfers between devices: 17.4 us -> none  [the longest x1 5.99 us: on_device(): lax.all_to_all(mixed_sum[None], 'seq', split_axis=1, concat_axis=0, tiled...]
    unnamed x34 -> x2, local copies, waits for them, and re-layouts: 19.6 us -> 3.51 us
    gather x6 -> x0, local copies, waits for them, and re-layouts: 13 us -> none  [the longest x1 4.33 us: on_device(): jnp.take(prefix_values.reshape(group_count, prefix_span, KV_HEADS, HD), k...]
    reduce_sum x8 -> x0, other arithmetic: 7.95 us -> none  [the longest x2 1.71 us: rms_scale(): jnp.mean(widened * widened, axis=-1, keepdims=True) + 1e-05]
  transfers between devices with their start and end apart: 3 -> 0, of which waited for: 0 -> 0; matrix products, arithmetic and copies ran while one was open for 30% -> 0% of each run, Pallas kernels for 0% -> 0%
where the time goes in v1:
time: 32.6 us; the launch traced here: 32.3 us
  Pallas kernels  26.2 us (80%)
  local copies, waits for them, and re-layouts  6.09 us (19%)
    pallas_call x1, Pallas kernels, on_device(): pl.pallas_call(functools.partial(kernel, n_seq, n_tp), out_shape=jax.Shap...  26.2 us
    unnamed x2, local copies, waits for them, and re-layouts  3.51 us
    reshape x1, local copies, waits for them, and re-layouts, on_device(): args[1] = args[1].reshape(1, width)  1.29 us
    reshape x1, local copies, waits for them, and re-layouts, on_device(): args[13] = args[13].reshape(1, width)  1.29 us

profile of v1, /device:TPU:0, one launch (start us, length us, event | category | flops | bytes accessed | tf_op | source)
XLA Modules:
  0.0 32.3 jit_solution(5082015025401075600)
XLA Ops:
  0.0 1.3 %reshape.6.attn_gain_h = f32[1,1152]{1,0:T(1,128)} reshape(f32[1152]{0:T(1024)} %param.18) | data formatting | bytes 9216 | tf_op jit(solution)/shard_map/reshape | solution.py:447
  1.3 1.3 %reshape.7.mlp_gain_h = f32[1,1152]{1,0:T(1,128)} reshape(f32[1152]{0:T(1024)} %param.30) | data formatting | bytes 9216 | tf_op jit(solution)/shard_map/reshape | solution.py:448
  2.6 2.2 %copy.18.w_query_h = bf16[1152,320]{1,0:T(8,128)(2,1)} copy(bf16[1152,320]{0,1:T(8,128)(2,1)} %param.19) | data formatting | bytes 1474560 | tf_op args[2]
  4.8 26.2 %shard_map.163 = bf16[8,1152]{1,0:T(8,128)(2,1)} custom-call(bf16[8,1152]{1,0:T(8,128)(2,1)} %tokens_h.1, f32[1,1152]{1,0:T(1,128)} %reshape.6.attn_gain_h, bf16[1152,320]{1,0:T(8,128)(2,1)} %copy.18.w_query_h, bf16[1152,384]{1,0:T(8,128)(2,1)} %w_key_h.1, bf16[1152,384]{1,0:T(8,128)(2,1)} %w_value_h.1, bf16[320,1152]{1,0:T(8,128)(2,1)} %w_out_h.1, ...), custom_call_target="tpu_custom_call" | custom-call | tf_op jit(solution)/shard_map/pallas_call | solution.py:452
  31.0 1.3 %copy.20 = bf16[8,1152]{1,0:T(8,128)(2,1)} copy(bf16[8,1152]{1,0:T(8,128)(2,1)} %shard_map.163) | data formatting | bytes 36864

commit v2 on v1

--- a/solution.py
+++ b/solution.py
@@ -66,20 +66,37 @@
         part = jnp.where(quarter == kv, mixed[s * rows : (s + 1) * rows], 0.0)
         part = part[:, :128] + part[:, 128:]
         both.append(part + pltpu.roll(part, HD, 1))
-    last = both[4]
+    top_row = jnp.zeros((rows, 128), F32)
+    total_row = jnp.zeros((rows, 128), F32)
     for s in range(5):
-        top = tops[s * rows : (s + 1) * rows]
-        total = totals[s * rows : (s + 1) * rows]
-        last = jnp.where(lanes == HD + s, top, last)
-        last = jnp.where(lanes == HD + 8 + s, total, last)
-    return jnp.concatenate(
-        [
-            jnp.where(lanes < HD, both[0], both[1]),
-            jnp.where(lanes < HD, both[2], both[3]),
-            jnp.where((lanes < HD) | (lanes < HD + 16), last, 0.0),
-        ],
-        axis=1,
-    )
+        top_row = jnp.where(lanes == HD + s, tops[s * rows : (s + 1) * rows], top_row)
+        total_row = jnp.where(lanes == HD + s, totals[s * rows : (s + 1) * rows], total_row)
+    blocks = [
+        jnp.where(lanes < HD, both[0], both[1]),
+        jnp.where(lanes < HD, both[2], both[3]),
+        jnp.where(lanes < HD, both[4], 0.0),
+    ]
+    return blocks, top_row, total_row
+
+
+def terms(x):
+    high = x.astype(BF16).astype(F32)
+    middle = (x - high).astype(BF16).astype(F32)
+    return high, middle, x - high - middle
+
+
+def fold_lanes(x):
+    out = x[:, :128]
+    for i in range(128, x.shape[1], 128):
+        out = out + x[:, i : i + 128]
+    return out
+
+
+def fold_max(x):
+    out = x[:, :128]
+    for i in range(128, x.shape[1], 128):
+        out = jnp.maximum(out, x[:, i : i + 128])
+    return out
 
 
 def column(ref, start, rows):
@@ -131,6 +148,7 @@
     queries,
     send_parts,
     parts,
+    all_scores,
     head_parts,
     down_parts,
     local_sem,
@@ -233,9 +251,9 @@
 
     copies["tokens"].wait()
     copies["attn_gain"].wait()
-    normed = rms(tokens[...], attn_gain[...])
+    normed = rms(tokens[...], attn_gain[...].reshape(1, tokens.shape[1]))
     copies["w_query"].wait()
-    q = dot(normed, w_query[...])
+    q = dot_t(normed, w_query[...])
     q = jnp.concatenate([q, jnp.zeros((rows, PACK - q.shape[1]), F32)], axis=1)
     q_own = rotate(q, cos3, sin3).astype(BF16)
     queries[seq] = q_own
@@ -301,7 +319,7 @@
     suf_mixed = dot(suf_weights.astype(BF16), suf_values[...].reshape(rows * suffix_span, WIDE))
     own_low = own_weight.astype(BF16).astype(F32)
     suf_mixed = suf_mixed + own_low * jnp.concatenate([new_values] * 5, axis=0)
-    suf_part = pack(suf_mixed, suf_top, suf_total, local_kv, rows)
+    suf_blocks, suf_end, suf_sum = pack(suf_mixed, suf_top, suf_total, local_kv, rows)
 
     over_peers(lambda k: seq_wait(queries, q_send, q_recv, k).wait_recv())
     for g in range(groups):
@@ -318,18 +336,23 @@
         group = column(group_of, c * chunk_rows, chunk_rows)
         group = jnp.concatenate([group] * 5, axis=0)
         mixed = jnp.zeros((5 * chunk_rows, WIDE), F32)
-        tops = jnp.full((5 * chunk_rows, 1), NEG, F32)
-        totals = jnp.zeros((5 * chunk_rows, 1), F32)
+        peaks = jnp.full((5 * chunk_rows, 128), NEG, F32)
         for g in range(groups):
             scores = jnp.where(spots < prefix_len[g], dot_t(q_all, keys[g]), NEG)
-            top = jnp.max(scores, axis=1, keepdims=True)
-            member = group == g
-            tops = jnp.where(member, top, tops)
-            weights = jnp.exp(scores - jnp.where(member, top, -NEG))
-            totals += jnp.sum(weights, axis=1, keepdims=True)
+            all_scores[g] = scores
+            peaks = jnp.where(group == g, fold_max(scores), peaks)
+        tops = jnp.max(peaks, axis=1, keepdims=True)
+        sums = jnp.zeros((5 * chunk_rows, 128), F32)
+        for g in range(groups):
+            weights = jnp.exp(all_scores[g] - jnp.where(group == g, tops, -NEG))
+            sums += fold_lanes(weights)
             mixed += dot(weights.astype(BF16), values[g])
-        packed = pack(mixed, tops, totals, local_kv, chunk_rows)
-        send_parts[pl.ds(c * per_chunk, per_chunk)] = packed.reshape(per_chunk, rows, PACK)
+        totals = jnp.sum(sums, axis=1, keepdims=True)
+        blocks, top_row, total_row = pack(mixed, tops, totals, local_kv, chunk_rows)
+        for i, term in enumerate(terms(top_row) + terms(total_row)):
+            blocks[2] = blocks[2] + (term if i == 0 else pltpu.roll(term, 8 * i, 1))
+        packed = jnp.concatenate(blocks, axis=1).reshape(per_chunk, rows, PACK)
+        send_parts[pl.ds(c * per_chunk, per_chunk)] = packed.astype(BF16)
         return carry
 
     if n_seq == per_chunk:
@@ -345,15 +368,15 @@
     parts[seq] = send_parts[seq]
     over_peers(lambda k: seq_wait(parts, p_send, p_recv, k).wait_recv())
 
-    every = parts[...]
-    ends = every[:, :, 256:]
-    suf_end = suf_part[:, 256:]
-    top = jnp.maximum(jnp.max(ends, axis=0), suf_end)
-    scales = jnp.exp(ends - top[None])
+    every = parts[...].astype(F32)
+    ends = every[:, :, 256:].reshape(n_seq * rows, 128)
+    rolled = [ends] + [pltpu.roll(ends, 128 - 8 * i, 1) for i in range(1, 6)]
+    part_tops = (rolled[0] + rolled[1] + rolled[2]).reshape(n_seq, rows, 128)
+    part_sums = (rolled[3] + rolled[4] + rolled[5]).reshape(n_seq, rows, 128)
+    top = jnp.maximum(jnp.max(part_tops, axis=0), suf_end)
+    scales = jnp.exp(part_tops - top[None])
     suf_scale = jnp.exp(suf_end - top)
-    total = suf_scale * pltpu.roll(suf_end, 120, 1)
-    for i in range(n_seq):
-        total = total + scales[i] * pltpu.roll(ends[i], 120, 1)
+    total = suf_scale * suf_sum + jnp.sum(scales * part_sums, axis=0)
     used_lane = lane_ids((rows, 128)) - HD < used
     share_of = jnp.where(used_lane, 1.0 / total, 0.0)
     half = lane_ids((rows, 128)) < HD
@@ -370,7 +393,7 @@
             axis=1,
         )
 
-    attended = weigh(suf_scale, suf_part)
+    attended = weigh(suf_scale, jnp.concatenate(suf_blocks, axis=1))
     for i in range(n_seq):
         attended = attended + weigh(scales[i], every[i])
     attended = attended[:, : 5 * HD].astype(BF16)
@@ -404,7 +427,7 @@
     head_parts[tp] = dot(attended, w_out[...]).astype(BF16)
     hidden = (tokens[...].astype(F32) + tp_sum(head_parts, h_send, h_recv)).astype(BF16)
     copies["mlp_gain"].wait()
-    mlp_in = rms(hidden, mlp_gain[...])
+    mlp_in = rms(hidden, mlp_gain[...].reshape(1, tokens.shape[1]))
     copies["w_gate"].wait()
     gate = dot(mlp_in, w_gate[...])
     copies["w_up"].wait()
@@ -444,8 +467,7 @@
     hidden_units = w_gate.shape[1]
     dma = pltpu.SemaphoreType.DMA
     args = list(args)
-    args[1] = args[1].reshape(1, width)
-    args[13] = args[13].reshape(1, width)
+    args[2] = w_query.T
     in_specs = [pl.BlockSpec(memory_space=pl.ANY)] * len(args)
     for i in (10, 11, 12):
         in_specs[i] = pl.BlockSpec(memory_space=pltpu.SMEM)
@@ -456,8 +478,8 @@
         out_specs=pl.BlockSpec(memory_space=pltpu.VMEM),
         scratch_shapes=[
             pltpu.VMEM((rows, width), BF16),
-            pltpu.VMEM((1, width), F32),
-            pltpu.VMEM(w_query.shape, BF16),
+            pltpu.VMEM((width,), F32),
+            pltpu.VMEM(w_query.shape[::-1], BF16),
             pltpu.VMEM((width, WIDE), BF16),
             pltpu.VMEM((width, WIDE), BF16),
             pltpu.VMEM(w_out.shape, BF16),
@@ -465,13 +487,14 @@
             pltpu.VMEM((groups, span, WIDE), BF16),
             pltpu.VMEM((rows, suffix.shape[1], WIDE), BF16),
             pltpu.VMEM((rows, suffix.shape[1], WIDE), BF16),
-            pltpu.VMEM((1, width), F32),
+            pltpu.VMEM((width,), F32),
             pltpu.VMEM(w_gate.shape, BF16),
             pltpu.VMEM(w_gate.shape, BF16),
             pltpu.VMEM(w_down.shape, BF16),
             pltpu.VMEM((n_seq, rows, PACK), BF16),
-            pltpu.VMEM((n_seq, rows, PACK), F32),
-            pltpu.VMEM((n_seq, rows, PACK), F32),
+            pltpu.VMEM((n_seq, rows, PACK), BF16),
+            pltpu.VMEM((n_seq, rows, PACK), BF16),
+            pltpu.VMEM((groups, 5 * rows * min(8, n_seq), span), F32),
             pltpu.VMEM((n_tp, rows, width), BF16),
             pltpu.VMEM((n_tp, rows, width), BF16),
             dma((12,)),

time: 32.6 us -> 29 us (0.89)
  local copies, waits for them, and re-layouts: 6.09 us -> 1.33 us
  Pallas kernels: 26.2 us -> 27.5 us
    reshape x2 -> x0, local copies, waits for them, and re-layouts: 2.58 us -> none  [the longest x1 1.29 us: on_device(): args[1] = args[1].reshape(1, width)]
    unnamed x2 -> x1, local copies, waits for them, and re-layouts: 3.51 us -> 1.33 us
    pallas_call x1, Pallas kernels: 26.2 us -> 27.5 us  [on_device(): pl.pallas_call(functools.partial(kernel, n_seq, n_tp), out_shape=jax.Shap...]
where the time goes in v2:
time: 29 us; the launch traced here: 28.8 us
  Pallas kernels  27.5 us (95%)
  local copies, waits for them, and re-layouts  1.33 us (5%)
    pallas_call x1, Pallas kernels, on_device(): pl.pallas_call(functools.partial(kernel, n_seq, n_tp), out_shape=jax.Shap...  27.5 us
    unnamed x1, local copies, waits for them, and re-layouts  1.33 us

profile of v2, /device:TPU:0, one launch (start us, length us, event | category | flops | bytes accessed | tf_op | source)
XLA Modules:
  0.0 28.8 jit_solution(10015154001700771822)
XLA Ops:
  0.0 27.5 %shard_map.163 = bf16[8,1152]{1,0:T(8,128)(2,1)} custom-call(bf16[8,1152]{1,0:T(8,128)(2,1)} %tokens_h.1, f32[1152]{0:T(1024)} %attn_gain_h.1, bf16[320,1152]{1,0:T(8,128)(2,1)} %bitcast.1, bf16[1152,384]{1,0:T(8,128)(2,1)} %w_key_h.1, bf16[1152,384]{1,0:T(8,128)(2,1)} %w_value_h.1, bf16[320,1152]{1,0:T(8,128)(2,1)} %w_out_h.1, ...), custom_call_target="tpu_custom_call" | custom-call | tf_op jit(solution)/shard_map/pallas_call | solution.py:474
  27.5 1.3 %copy.19 = bf16[8,1152]{1,0:T(8,128)(2,1)} copy(bf16[8,1152]{1,0:T(8,128)(2,1)} %shard_map.163) | data formatting | bytes 36864

commit v3 on v2

--- a/solution.py
+++ b/solution.py
@@ -148,7 +148,6 @@
     queries,
     send_parts,
     parts,
-    all_scores,
     head_parts,
     down_parts,
     local_sem,
@@ -336,15 +335,14 @@
         group = column(group_of, c * chunk_rows, chunk_rows)
         group = jnp.concatenate([group] * 5, axis=0)
         mixed = jnp.zeros((5 * chunk_rows, WIDE), F32)
-        peaks = jnp.full((5 * chunk_rows, 128), NEG, F32)
+        tops = jnp.full((5 * chunk_rows, 1), NEG, F32)
+        sums = jnp.zeros((5 * chunk_rows, 128), F32)
         for g in range(groups):
             scores = jnp.where(spots < prefix_len[g], dot_t(q_all, keys[g]), NEG)
-            all_scores[g] = scores
-            peaks = jnp.where(group == g, fold_max(scores), peaks)
-        tops = jnp.max(peaks, axis=1, keepdims=True)
-        sums = jnp.zeros((5 * chunk_rows, 128), F32)
-        for g in range(groups):
-            weights = jnp.exp(all_scores[g] - jnp.where(group == g, tops, -NEG))
+            top = jnp.max(fold_max(scores), axis=1, keepdims=True)
+            member = group == g
+            tops = jnp.where(member, top, tops)
+            weights = jnp.exp(scores - jnp.where(member, top, -NEG))
             sums += fold_lanes(weights)
             mixed += dot(weights.astype(BF16), values[g])
         totals = jnp.sum(sums, axis=1, keepdims=True)
@@ -494,7 +492,6 @@
             pltpu.VMEM((n_seq, rows, PACK), BF16),
             pltpu.VMEM((n_seq, rows, PACK), BF16),
             pltpu.VMEM((n_seq, rows, PACK), BF16),
-            pltpu.VMEM((groups, 5 * rows * min(8, n_seq), span), F32),
             pltpu.VMEM((n_tp, rows, width), BF16),
             pltpu.VMEM((n_tp, rows, width), BF16),
             dma((12,)),

time: 29 us -> 28 us (0.966)
  Pallas kernels: 27.5 us -> 26.5 us
    pallas_call x1, Pallas kernels: 27.5 us -> 26.5 us  [on_device(): pl.pallas_call(functools.partial(kernel, n_seq, n_tp), out_shape=jax.Shap...]
where the time goes in v3:
time: 28 us; the launch traced here: 27.8 us
  Pallas kernels  26.5 us (95%)
  local copies, waits for them, and re-layouts  1.33 us (5%)
    pallas_call x1, Pallas kernels, on_device(): pl.pallas_call(functools.partial(kernel, n_seq, n_tp), out_shape=jax.Shap...  26.5 us
    unnamed x1, local copies, waits for them, and re-layouts  1.33 us

profile of v3, /device:TPU:0, one launch (start us, length us, event | category | flops | bytes accessed | tf_op | source)
XLA Modules:
  0.0 27.8 jit_solution(17300335355943291368)
XLA Ops:
  0.0 26.5 %shard_map.163 = bf16[8,1152]{1,0:T(8,128)(2,1)} custom-call(bf16[8,1152]{1,0:T(8,128)(2,1)} %tokens_h.1, f32[1152]{0:T(1024)} %attn_gain_h.1, bf16[320,1152]{1,0:T(8,128)(2,1)} %bitcast.1, bf16[1152,384]{1,0:T(8,128)(2,1)} %w_key_h.1, bf16[1152,384]{1,0:T(8,128)(2,1)} %w_value_h.1, bf16[320,1152]{1,0:T(8,128)(2,1)} %w_out_h.1, ...), custom_call_target="tpu_custom_call" | custom-call | tf_op jit(solution)/shard_map/pallas_call | solution.py:472
  26.5 1.3 %copy.19 = bf16[8,1152]{1,0:T(8,128)(2,1)} copy(bf16[8,1152]{1,0:T(8,128)(2,1)} %shard_map.163) | data formatting | bytes 36864

commit v4 on v3

--- a/solution.py
+++ b/solution.py
@@ -396,34 +396,38 @@
         attended = attended + weigh(scales[i], every[i])
     attended = attended[:, : 5 * HD].astype(BF16)
 
-    def tp_sum(buf, send, recv):
-        for k in range(1, n_tp):
-            pltpu.make_async_remote_copy(
-                src_ref=buf.at[tp],
-                dst_ref=buf.at[tp],
-                send_sem=send.at[k],
-                recv_sem=recv.at[tp],
-                device_id={"tp": lax.rem(tp + k, n_tp)},
-                device_id_type=MESH,
-            ).start()
-        for k in range(1, n_tp):
-            other = lax.rem(tp + k, n_tp)
-            pltpu.make_async_remote_copy(
-                src_ref=buf.at[other],
-                dst_ref=buf.at[other],
-                send_sem=send.at[k],
-                recv_sem=recv.at[other],
-                device_id={"tp": other},
-                device_id_type=MESH,
-            ).wait_recv()
+    width = tokens.shape[1]
+    cut = 512 if width > 512 else width
+    pieces = [(0, cut)] + ([(cut, width - cut)] if width > cut else [])
+
+    def tp_copy(buf, send, recv, k, c, owner):
+        piece = buf.at[owner, :, pl.ds(*pieces[c])]
+        return pltpu.make_async_remote_copy(
+            src_ref=piece,
+            dst_ref=piece,
+            send_sem=send.at[c, k],
+            recv_sem=recv.at[c, owner],
+            device_id={"tp": lax.rem(tp + k, n_tp)},
+            device_id_type=MESH,
+        )
+
+    def tp_sum(left, weight, buf, send, recv):
+        for c, (start, size) in enumerate(pieces):
+            piece = dot(left, weight[:, start : start + size]).astype(BF16)
+            buf[tp, :, start : start + size] = piece
+            for k in range(1, n_tp):
+                tp_copy(buf, send, recv, k, c, tp).start()
+        for c in range(len(pieces)):
+            for k in range(1, n_tp):
+                tp_copy(buf, send, recv, k, c, lax.rem(tp + k, n_tp)).wait_recv()
         total = buf[0].astype(F32)
         for i in range(1, n_tp):
             total = total + buf[i].astype(F32)
         return total
 
     copies["w_out"].wait()
-    head_parts[tp] = dot(attended, w_out[...]).astype(BF16)
-    hidden = (tokens[...].astype(F32) + tp_sum(head_parts, h_send, h_recv)).astype(BF16)
+    total = tp_sum(attended, w_out, head_parts, h_send, h_recv)
+    hidden = (tokens[...].astype(F32) + total).astype(BF16)
     copies["mlp_gain"].wait()
     mlp_in = rms(hidden, mlp_gain[...].reshape(1, tokens.shape[1]))
     copies["w_gate"].wait()
@@ -432,8 +436,7 @@
     up = dot(mlp_in, w_up[...])
     activation = (gate / (1.0 + jnp.exp(-gate)) * up).astype(BF16)
     copies["w_down"].wait()
-    down_parts[tp] = dot(activation, w_down[...]).astype(BF16)
-    total = tp_sum(down_parts, d_send, d_recv)
+    total = tp_sum(activation, w_down, down_parts, d_send, d_recv)
     out_ref[...] = (hidden.astype(F32) + total).astype(BF16)
 
     over_peers(
@@ -446,15 +449,9 @@
 
     over_peers(sent_part)
     for buf, send, recv in ((head_parts, h_send, h_recv), (down_parts, d_send, d_recv)):
-        for k in range(1, n_tp):
-            pltpu.make_async_remote_copy(
-                src_ref=buf.at[tp],
-                dst_ref=buf.at[tp],
-                send_sem=send.at[k],
-                recv_sem=recv.at[tp],
-                device_id={"tp": lax.rem(tp + k, n_tp)},
-                device_id_type=MESH,
-            ).wait_send()
+        for c in range(len(pieces)):
+            for k in range(1, n_tp):
+                tp_copy(buf, send, recv, k, c, tp).wait_send()
 
 
 def on_device(n_seq, n_tp, *args):
@@ -500,10 +497,10 @@
             dma((n_seq,)),
             dma((n_seq,)),
             dma((n_seq,)),
-            dma((n_tp,)),
-            dma((n_tp,)),
-            dma((n_tp,)),
-            dma((n_tp,)),
+            dma((2, n_tp)),
+            dma((2, n_tp)),
+            dma((2, n_tp)),
+            dma((2, n_tp)),
         ],
         compiler_params=pltpu.CompilerParams(
             collective_id=0, has_side_effects=True, vmem_limit_bytes=56 * 1024 * 1024

time: 28 us -> 28.2 us (level)
  no operation moved by 1% of the time
where the time goes in v4:
time: 28.2 us; the launch traced here: 28 us
  Pallas kernels  26.7 us (95%)
  local copies, waits for them, and re-layouts  1.33 us (5%)
    pallas_call x1, Pallas kernels, on_device(): pl.pallas_call(functools.partial(kernel, n_seq, n_tp), out_shape=jax.Shap...  26.7 us
    unnamed x1, local copies, waits for them, and re-layouts  1.33 us

profile of v4, /device:TPU:0, one launch (start us, length us, event | category | flops | bytes accessed | tf_op | source)
XLA Modules:
  0.0 28.0 jit_solution(14062128412496959716)
XLA Ops:
  0.0 26.7 %shard_map.163 = bf16[8,1152]{1,0:T(8,128)(2,1)} custom-call(bf16[8,1152]{1,0:T(8,128)(2,1)} %tokens_h.1, f32[1152]{0:T(1024)} %attn_gain_h.1, bf16[320,1152]{1,0:T(8,128)(2,1)} %bitcast.1, bf16[1152,384]{1,0:T(8,128)(2,1)} %w_key_h.1, bf16[1152,384]{1,0:T(8,128)(2,1)} %w_value_h.1, bf16[320,1152]{1,0:T(8,128)(2,1)} %w_out_h.1, ...), custom_call_target="tpu_custom_call" | custom-call | tf_op jit(solution)/shard_map/pallas_call | solution.py:469
  26.7 1.3 %copy.19 = bf16[8,1152]{1,0:T(8,128)(2,1)} copy(bf16[8,1152]{1,0:T(8,128)(2,1)} %shard_map.163) | data formatting | bytes 36864
